TPU v7x, 32 devices: a whole 2x2x4 slice. The times are simulated.
32 devices in a mesh: row: 2 (over x), col: 4 (over y, core), feat: 4 (over z).
Axes of the slice: x: 2, y: 2, z: 4, core: 2. Of those that a mesh axis runs over, the one named last changes fastest.
Arguments:
- features: bfloat16 [65536, 128], P(('row', 'col'), 'feat'), may hold values from -6 to 6
- tiles: bfloat16 [2, 4, 1536, 128, 128], P('row', 'col', 'feat'), may hold values from 0 to 0.04321289
- tile_row: int32 [2, 4, 1536], P('row', 'col', 'feat'), may hold values from 0 to 255
- tile_col: int32 [2, 4, 1536], P('row', 'col', 'feat'), may hold values from 0 to 127
- tile_count: int32 [2, 4, 4], P('row', 'col', 'feat'), may hold values from 1 to 384, as said below
- weight: bfloat16 [128, 256], replicated, may hold values from -0.5 to 0.5
- bias: float32 [256], replicated, may hold values from -3 to 3
Outputs:
- output: bfloat16 [65536, 256], P(('row', 'col', 'feat'))
Inputs may be any that keep to these rules, and one draw needn't show every extreme that they name: `tile_count`: some device has all 384 slots live.
All inputs are finite; a program needn't handle non-finite values.
Results may differ from a plain program's by a relative error of at most 0.02.
Values may be sent and summed in bfloat16 or wider, within the bound.
A program may use at most 128 MiB of HBM per device.

v0:
```python
import jax
import jax.numpy as jnp
from jax import lax
from jax.sharding import PartitionSpec as P


def body(features, tiles, tile_row, tile_col, tile_count, weight, bias):
    node_rows = lax.all_to_all(features, "feat", split_axis=0, concat_axis=1, tiled=True)
    sources = lax.all_gather(node_rows, ("row", "feat"), axis=0, tiled=True)
    tile_side = tiles.shape[-1]
    width = sources.shape[1]
    node_dev = features.shape[0] // lax.axis_size("feat")
    block_rows = lax.axis_size("col") * lax.axis_size("feat") * node_dev // tile_side
    src_blocks = sources.reshape(-1, tile_side, width)
    slot_total = tiles.shape[2]
    tile_stack = tiles.reshape(slot_total, tile_side, tile_side)
    row_index = tile_row.reshape(slot_total)
    col_index = tile_col.reshape(slot_total)
    live_count = tile_count.reshape(())
    block = min(32, slot_total)
    turns = (live_count + block - 1) // block

    def one_turn(turn, partial_value):
        start = turn * block
        tile_block = lax.dynamic_slice_in_dim(tile_stack, start, block, 0)
        rows_here = lax.dynamic_slice_in_dim(row_index, start, block, 0)
        cols_here = lax.dynamic_slice_in_dim(col_index, start, block, 0)
        picked = jnp.take(src_blocks, cols_here, axis=0)
        prods = jnp.einsum("tij,tjf->tif", tile_block, picked, preferred_element_type=jnp.float32)
        live = start + jnp.arange(block, dtype=jnp.int32) < live_count
        prods = jnp.where(live[:, None, None], prods, jnp.zeros_like(prods))
        return partial_value.at[rows_here].add(prods)

    empty = jnp.zeros((block_rows, tile_side, width), jnp.float32)
    partial_value = lax.fori_loop(0, turns, one_turn, empty)
    rounded = lax.optimization_barrier(
        partial_value.reshape(block_rows * tile_side, width).astype(jnp.bfloat16)
    )
    terms = rounded.astype(jnp.float32)
    agg = lax.psum_scatter(
        terms.astype(jnp.bfloat16), ("col", "feat"), scatter_dimension=0, tiled=True
    )
    hidden = jnp.dot(agg, weight, preferred_element_type=jnp.float32) + bias
    return jax.nn.relu(hidden).astype(jnp.bfloat16)


def solution(mesh):
    placed = (
        P(("row", "col"), "feat"),
        P("row", "col", "feat", None, None),
        P("row", "col", "feat"),
        P("row", "col", "feat"),
        P("row", "col", "feat"),
        P(),
        P(),
    )
    return jax.shard_map(
        body, mesh=mesh, in_specs=placed, out_specs=P(("row", "col", "feat"), None), check_vma=False
    )
```

profile of v0, /device:TPU:0, one launch (start us, length us, event | category | flops | bytes accessed | tf_op | source)
XLA Modules:
  0.0 376.8 jit_solution(6807245090565049449)
XLA Ops:
  6.5 1.1 copy.17
  7.7 20.7 %all_to_all.19 = bf16[4,2048,32]{1,2,0:T(8,128)(2,1)} all-to-all(bf16[4,2048,32]{1,2,0:T(8,128)(2,1)S(1)} %bitcast.18), channel_id=1, replica_groups=mesh['row'=2,'col'=4,'feat'=4] {'feat'}, dimensions={0} | all-to-all | bytes 1048576 | tf_op jit(solution)/shard_map/all_to_all | solution.py:8
  29.1 0.7 reduce
  29.8 0.7 reduce.1
  30.5 70.5 %all-gather.2.cloned.1.call-done = bf16[16384,128]{0,1:T(8,128)(2,1)} async-done(((bf16[2048,128]{0,1:T(8,128)(2,1)}), bf16[16384,128]{0,1:T(8,128)(2,1)}) %all-gather.2.cloned.1.call-update) | async-done | bytes 4194320 | tf_op jit(solution)/shard_map/all_gather | solution.py:9
  101.0 6.4 %copy.14 = bf16[16384,128]{1,0:T(8,128)(2,1)} copy(bf16[16384,128]{0,1:T(8,128)(2,1)} %all-gather.2.cloned.1.call-done) | data formatting | bytes 8388608 | tf_op jit(solution)/shard_map/while | solution.py:35
  107.4 7.8 %broadcast_in_dim.28 = f32[256,128,128]{2,1,0:T(8,128)} broadcast(f32[]{:T(128)} %constant.47.clone.1), dimensions={} | broadcast | bytes 16777220 | tf_op jit(solution)/shard_map/broadcast_in_dim | solution.py:34
  115.3 34.9 %while.10 = (s32[]{:T(128)}, f32[256,128,128]{2,1,0:T(8,128)}, s32[]{:T(128)}, s32[384]{0:T(512)S(1)}, s32[]{:T(128)}, /*index=5*/bf16[384,128,128]{2,1,0:T(8,12...) while((s32[]{:T(128)}, f32[256,128,128]{2,1,0:T(8,128)}, ...), condition=%wide.region_2.3_spmd, body=%wide.region_0.2_spmd.sunk | while | flops 135791968 | bytes 12588215 | solution.py:35
  115.3 0.1 compare_select_fusion.4
  115.4 0.7 compare_and_fusion.2
  116.1 2.9 gather_fusion
  119.0 1.7 convolution_select_fusion.2
  120.8 6.1 %scatter_fusion = f32[256,128,128]{2,1,0:T(8,128)} fusion(f32[256,128,128]{2,1,0:T(8,128)} %get-tuple-element.161, s32[32]{0:T(128)S(1)} %compare_select_fusion.4, f32[32,128,128]{2,1,0:T(8,128)S(1)} %convolution_select_fusion.2), kind=kCustom, calls=%fused_computation.1.clone.1 | custom fusion | flops 524288 | bytes 6291584 | tf_op jit(solution)/shard_map/while/body/scatter-add | solution.py:32
  127.0 0.7 compare_and_fusion.2
  127.7 2.9 gather_fusion
  130.6 1.7 convolution_select_fusion.2
  132.4 6.1 %scatter_fusion = f32[256,128,128]{2,1,0:T(8,128)} fusion(f32[256,128,128]{2,1,0:T(8,128)} %get-tuple-element.161, s32[32]{0:T(128)S(1)} %compare_select_fusion.4, f32[32,128,128]{2,1,0:T(8,128)S(1)} %convolution_select_fusion.2), kind=kCustom, calls=%fused_computation.1.clone.1 | custom fusion | flops 524288 | bytes 6291584 | tf_op jit(solution)/shard_map/while/body/scatter-add | solution.py:32
  138.6 0.7 compare_and_fusion.2
  139.3 2.9 gather_fusion
  142.3 1.7 convolution_select_fusion.2
  144.0 6.1 %scatter_fusion = f32[256,128,128]{2,1,0:T(8,128)} fusion(f32[256,128,128]{2,1,0:T(8,128)} %get-tuple-element.161, s32[32]{0:T(128)S(1)} %compare_select_fusion.4, f32[32,128,128]{2,1,0:T(8,128)S(1)} %convolution_select_fusion.2), kind=kCustom, calls=%fused_computation.1.clone.1 | custom fusion | flops 524288 | bytes 6291584 | tf_op jit(solution)/shard_map/while/body/scatter-add | solution.py:32
  150.1 9.2 %convert_element_type.11 = bf16[256,128,128]{2,1,0:T(8,128)(2,1)} convert(f32[256,128,128]{2,1,0:T(8,128)} %get-tuple-element.48) | non-fusion elementwise | flops 4194304 | bytes 25165824 | tf_op jit(solution)/shard_map/convert_element_type | solution.py:37
  159.4 208.2 %reduce-scatter.2.cloned.1.call-done = bf16[2048,128]{1,0:T(8,128)(2,1)} async-done(((bf16[32768,128]{1,0:T(8,128)(2,1)}), bf16[2048,128]{1,0:T(8,128)(2,1)}) %reduce-scatter.2.cloned.1.call-update) | async-done | bytes 524304 | tf_op jit(solution)/shard_map/reduce_scatter | solution.py:40
  367.6 2.4 fusion.7
  (13 shorter events, 0.3 us)
Async XLA Ops:
  6.5 361.0 %copy-start = (bf16[128,256]{1,0:T(8,128)(2,1)S(1)}, bf16[128,256]{1,0:T(8,128)(2,1)}, u32[]{:S(2)}) copy-start(bf16[128,256]{1,0:T(8,128)(2,1)} %param.14) | copy-start | bytes 196612
  6.5 94.5 %all-gather.2.cloned.1.call-start = ((), (), s32[]{:S(2)}) async-start(), calls=%async_computation.2 | async-start | bytes 4718592 | tf_op jit(solution)/shard_map/all_gather | solution.py:9
  28.4 339.2 %reduce-scatter.2.cloned.1.call-start = ((), (), s32[]{:S(2)}) async-start(), calls=%async_computation.3 | async-start | bytes 8912896 | tf_op jit(solution)/shard_map/reduce_scatter | solution.py:40
  159.3 208.2 %copy-start.1 = (f32[256]{0:T(256)S(1)}, f32[256]{0:T(256)}, u32[]{:S(2)}) copy-start(f32[256]{0:T(256)} %param.15) | copy-start | bytes 3076
Sparse Core Ops, SparseCore 0:
  28.5 72.4 all-gather.1
  159.5 208.0 reduce-scatter.1
where the time goes:
time: 380 us; the launch traced here: 377 us
  waiting for transfers between devices  279 us (73%)
  other arithmetic  31.4 us (8%)
  local copies, waits for them, and re-layouts  24.2 us (6%)
  blocking collectives  20.7 us (5%)
  between operations  14.1 us (4%)
  matrix products  7.64 us (2%)
    reduce_scatter x1, waiting for transfers between devices, body(): lax.psum_scatter(terms.astype(jnp.bfloat16), ('col', 'feat'), scatter_dim...  208 us
    all_gather x1, waiting for transfers between devices, body(): sources = lax.all_gather(node_rows, ('row', 'feat'), axis=0, tiled=True)  70.5 us
    all_to_all x1, blocking collectives, body(): lax.all_to_all(features, 'feat', split_axis=0, concat_axis=1, tiled=True)  20.7 us
    scatter-add x3, other arithmetic, one_turn(): return partial_value.at[rows_here].add(prods)  18.4 us
    convert_element_type x1, other arithmetic, body(): partial_value.reshape(block_rows * tile_side, width).astype(jnp.bfloat16)  9.2 us
    gather x3, local copies, waits for them, and re-layouts, one_turn(): picked = jnp.take(src_blocks, cols_here, axis=0)  8.81 us
    broadcast_in_dim x1, local copies, waits for them, and re-layouts, body(): empty = jnp.zeros((block_rows, tile_side, width), jnp.float32)  7.85 us
  transfers between devices with their start and end apart: 2, of which 2 were waited for; matrix products, arithmetic and copies ran while one was open for 0% of the time, Pallas kernels for 0%

commit v1 on v0

v1 whole, which is shorter than its diff:
```python
import functools

import jax
import jax.numpy as jnp
from jax import lax
from jax.experimental import pallas as pl
from jax.experimental.pallas import tpu as pltpu
from jax.sharding import PartitionSpec as P

MESH = pl.DeviceIdType.MESH
MIB = 1 << 20


def gather_kernel(n_row, n_feat, parts, own_ref, out_ref, local_sem, z_send, z_recv, x_send, x_recv):
    r = lax.axis_index("row")
    f = lax.axis_index("feat")
    blocks, width = own_ref.shape[0], own_ref.shape[1]
    step = blocks // parts

    barrier = pltpu.get_barrier_semaphore()
    for p in range(1, n_row):
        pl.semaphore_signal(barrier, inc=1, device_id={"row": lax.rem(r + p, n_row)}, device_id_type=MESH)

    @pl.when(f > 0)
    def _():
        pl.semaphore_signal(barrier, inc=1, device_id={"feat": f - 1}, device_id_type=MESH)

    @pl.when(f < n_feat - 1)
    def _():
        pl.semaphore_signal(barrier, inc=1, device_id={"feat": f + 1}, device_id_type=MESH)

    ends = jnp.where(f > 0, 1, 0) + jnp.where(f < n_feat - 1, 1, 0)
    pl.semaphore_wait(barrier, n_row - 1 + ends)

    def region(row, feat, c):
        return out_ref.at[pl.ds(row * blocks + c * step, step), pl.ds(pl.multiple_of(feat * width, width), width), :]

    def own(c):
        return own_ref.at[pl.ds(c * step, step)]

    def along(way, hop, c, origin, src=None):
        target = f + 1 if way == 0 else f - 1
        place = region(r, origin, c)
        return pltpu.make_async_remote_copy(
            src_ref=place if src is None else src, dst_ref=place,
            send_sem=z_send.at[way, hop, c], recv_sem=z_recv.at[way, hop, c],
            device_id={"feat": target}, device_id_type=MESH)

    def across(p, origin, c, src=None):
        place = region(r, origin, c)
        return pltpu.make_async_remote_copy(
            src_ref=place if src is None else src, dst_ref=place,
            send_sem=x_send.at[p - 1, origin, c], recv_sem=x_recv.at[p - 1, origin, c],
            device_id={"row": lax.rem(r + p, n_row)}, device_id_type=MESH)

    for c in range(parts):
        @pl.when(f < n_feat - 1)
        def _():
            along(0, 0, c, f, own(c)).start()

        @pl.when(f > 0)
        def _():
            along(1, 0, c, f, own(c)).start()

        for p in range(1, n_row):
            across(p, f, c, own(c)).start()
    local = pltpu.make_async_copy(own_ref, out_ref.at[pl.ds(r * blocks, blocks), pl.ds(pl.multiple_of(f * width, width), width), :], local_sem)
    local.start()

    for hop in range(1, n_feat):
        for c in range(parts):
            @pl.when(f - hop >= 0)
            def _():
                origin = f - hop
                along(0, hop - 1, c, origin).wait_recv()
                if hop < n_feat - 1:
                    @pl.when(f < n_feat - 1)
                    def _():
                        along(0, hop, c, origin).start()
                for p in range(1, n_row):
                    across(p, origin, c).start()

            @pl.when(f + hop < n_feat)
            def _():
                origin = f + hop
                along(1, hop - 1, c, origin).wait_recv()
                if hop < n_feat - 1:
                    @pl.when(f > 0)
                    def _():
                        along(1, hop, c, origin).start()
                for p in range(1, n_row):
                    across(p, origin, c).start()

    for origin in range(n_feat):
        for c in range(parts):
            for p in range(1, n_row):
                across(p, origin, c).wait()
    for hop in range(n_feat - 1):
        for c in range(parts):
            @pl.when((f < n_feat - 1) & (f - hop >= 0))
            def _():
                along(0, hop, c, f - hop).wait_send()

            @pl.when((f > 0) & (f + hop < n_feat))
            def _():
                along(1, hop, c, f + hop).wait_send()
    local.wait()


def tile_kernel(chunk, unroll, brows, count_ref, row_ref, col_ref, src_ref, tiles_ref, out_ref, acc, stage, sems):
    i = pl.program_id(0)
    count = count_ref[0]

    @pl.when(i == 0)
    def _():
        def clear(b, carry):
            acc[b] = jnp.zeros(acc.shape[1:], jnp.float32)
            return carry
        lax.fori_loop(0, brows, clear, 0)

    left = count - i * chunk
    turns = jnp.clip((left + unroll - 1) // unroll, 0, chunk // unroll)

    def turn(t, carry):
        for u in range(unroll):
            s = t * unroll + u
            k = i * chunk + s
            row = jnp.where(k < count, row_ref[k], brows)
            acc[row] += lax.dot_general(
                tiles_ref[s], src_ref[col_ref[k]], (((1,), (1,)), ((), ())), preferred_element_type=jnp.float32)
        return carry

    lax.fori_loop(0, turns, turn, 0)

    @pl.when(i == pl.num_programs(0) - 1)
    def _():
        size = stage.shape[1]
        total = brows // size
        def put(n):
            return pltpu.make_async_copy(stage.at[n % 2], out_ref.at[pl.ds(n * size, size)], sems.at[n % 2])
        for n in range(total):
            if n >= 2:
                put(n - 2).wait()
            def cast(b, carry):
                stage[n % 2, b] = acc[n * size + b].astype(jnp.bfloat16)
                return carry
            lax.fori_loop(0, size, cast, 0)
            put(n).start()
        for n in range(max(0, total - 2), total):
            put(n).wait()


def reduce_kernel(n_feat, parts, part_ref, weight_ref, bias_ref, out_ref,
                  own_a, own_b, got_a, got_b, y_out, y_in, z_out, z_in,
                  local_sem, a_send, a_recv, b_send, b_recv, y_send, y_recv, z_send, z_recv):
    c = lax.axis_index("col")
    f = lax.axis_index("feat")
    hi, core = c // 2, lax.rem(c, 2)
    mate = {"col": hi * 2 + (1 - core)}
    over = {"col": (1 - hi) * 2 + core}
    size = got_a.shape[2]

    barrier = pltpu.get_barrier_semaphore()
    for target in (mate, over):
        pl.semaphore_signal(barrier, inc=1, device_id=target, device_id_type=MESH)
    for d in range(1, n_feat):
        pl.semaphore_signal(barrier, inc=1, device_id={"feat": lax.rem(f + d, n_feat)}, device_id_type=MESH)
    pl.semaphore_wait(barrier, n_feat + 1)

    load_a = pltpu.make_async_copy(part_ref.at[1 - hi, core], own_a, local_sem.at[0])
    load_b = pltpu.make_async_copy(part_ref.at[hi, core], own_b, local_sem.at[1])
    load_a.start()

    def rows(t):
        return pl.ds(pl.multiple_of(t * size, size), size)

    def pair_a(t):
        return pltpu.make_async_remote_copy(
            src_ref=part_ref.at[1 - hi, 1 - core, :, rows(t), :], dst_ref=got_a.at[t],
            send_sem=a_send.at[t], recv_sem=a_recv.at[t], device_id=mate, device_id_type=MESH)

    def pair_b(t):
        return pltpu.make_async_remote_copy(
            src_ref=part_ref.at[hi, 1 - core, :, rows(t), :], dst_ref=got_b.at[t],
            send_sem=b_send.at[t], recv_sem=b_recv.at[t], device_id=mate, device_id_type=MESH)

    def swap_y(t):
        return pltpu.make_async_remote_copy(
            src_ref=y_out.at[t], dst_ref=y_in.at[t],
            send_sem=y_send.at[t], recv_sem=y_recv.at[t], device_id=over, device_id_type=MESH)

    def swap_z(t, d):
        target = lax.rem(f + d, n_feat)
        return pltpu.make_async_remote_copy(
            src_ref=z_out.at[t, target], dst_ref=z_in.at[t, d - 1],
            send_sem=z_send.at[t, d - 1], recv_sem=z_recv.at[t, d - 1],
            device_id={"feat": target}, device_id_type=MESH)

    def start_a(t, carry):
        pair_a(t).start()
        return carry

    lax.fori_loop(0, parts, start_a, 0)
    load_b.start()
    load_a.wait()
    load_b.wait()

    def turn(t, carry):
        @pl.when(t < parts)
        def _():
            pair_b(t).start()
            pair_a(t).wait_recv()
            for g in range(n_feat):
                y_out[t, g] = (own_a[g, rows(t), :].astype(jnp.float32) + got_a[t, g].astype(jnp.float32)).astype(jnp.bfloat16)
            swap_y(t).start()

        @pl.when((t >= 1) & (t < parts + 1))
        def _():
            s = t - 1
            pair_b(s).wait_recv()
            swap_y(s).wait_recv()
            for g in range(n_feat):
                z_out[s, g] = (own_b[g, rows(s), :].astype(jnp.float32) + got_b[s, g].astype(jnp.float32)
                               + y_in[s, g].astype(jnp.float32)).astype(jnp.bfloat16)
            for d in range(1, n_feat):
                swap_z(s, d).start()

        @pl.when(t >= 2)
        def _():
            s = t - 2
            total = z_out[s, f].astype(jnp.float32)
            for d in range(1, n_feat):
                swap_z(s, d).wait_recv()
                total += z_in[s, d - 1].astype(jnp.float32)
            hidden = jnp.dot(total.astype(jnp.bfloat16), weight_ref[...], preferred_element_type=jnp.float32)
            out_ref[rows(s), :] = jnp.maximum(hidden + bias_ref[...], 0.0).astype(jnp.bfloat16)
        return carry

    lax.fori_loop(0, parts + 2, turn, 0)

    def drain(t, carry):
        pair_a(t).wait_send()
        pair_b(t).wait_send()
        swap_y(t).wait_send()
        for d in range(1, n_feat):
            swap_z(t, d).wait_send()
        return carry

    lax.fori_loop(0, parts, drain, 0)


def body(n_row, n_col, n_feat, features, tiles, tile_row, tile_col, tile_count, weight, bias):
    side = tiles.shape[-1]
    slots = tiles.shape[2]
    held, width = features.shape
    fan = weight.shape[0]
    hidden = weight.shape[1]
    node_dev = held // n_feat
    brows = n_col * n_feat * node_dev // side
    blocks = held // side
    any_spec = pl.BlockSpec(memory_space=pl.ANY)
    vmem_spec = pl.BlockSpec(memory_space=pltpu.VMEM)
    dma = pltpu.SemaphoreType.DMA

    own = features.reshape(blocks, side, width).transpose(0, 2, 1)
    parts = 4
    sources = pl.pallas_call(
        functools.partial(gather_kernel, n_row, n_feat, parts),
        out_shape=jax.ShapeDtypeStruct((n_row * blocks, fan, side), jnp.bfloat16),
        in_specs=[any_spec],
        out_specs=any_spec,
        scratch_shapes=[
            dma, dma((2, n_feat - 1, parts)), dma((2, n_feat - 1, parts)),
            dma((n_row - 1, n_feat, parts)), dma((n_row - 1, n_feat, parts)),
        ],
        compiler_params=pltpu.CompilerParams(collective_id=0, has_side_effects=True),
        name="gather_sources",
    )(own)

    chunk, unroll = 32, 8
    partial_value = pl.pallas_call(
        functools.partial(tile_kernel, chunk, unroll, brows),
        out_shape=jax.ShapeDtypeStruct((brows, side, fan), jnp.bfloat16),
        grid_spec=pltpu.PrefetchScalarGridSpec(
            num_scalar_prefetch=3,
            grid=(slots // chunk,),
            in_specs=[
                pl.BlockSpec((n_row * blocks, fan, side), lambda i, n, rows, cols: (0, 0, 0), pipeline_mode=pl.Buffered(1)),
                pl.BlockSpec((chunk, side, side), lambda i, n, rows, cols: (jnp.minimum(i, (n[0] - 1) // chunk), 0, 0)),
            ],
            out_specs=any_spec,
            scratch_shapes=[
                pltpu.VMEM((brows + 1, side, fan), jnp.float32),
                pltpu.VMEM((2, 32, side, fan), jnp.bfloat16),
                dma((2,)),
            ],
        ),
        compiler_params=pltpu.CompilerParams(vmem_limit_bytes=48 * MIB),
        name="tile_products",
    )(tile_count.reshape(1), tile_row.reshape(slots), tile_col.reshape(slots), sources, tiles.reshape(slots, side, side))

    size = 128
    parts = node_dev // size
    bf = jnp.bfloat16
    return pl.pallas_call(
        functools.partial(reduce_kernel, n_feat, parts),
        out_shape=jax.ShapeDtypeStruct((node_dev, hidden), bf),
        in_specs=[any_spec, vmem_spec, vmem_spec],
        out_specs=vmem_spec,
        scratch_shapes=[
            pltpu.VMEM((n_feat, node_dev, fan), bf),
            pltpu.VMEM((n_feat, node_dev, fan), bf),
            pltpu.VMEM((parts, n_feat, size, fan), bf),
            pltpu.VMEM((parts, n_feat, size, fan), bf),
            pltpu.VMEM((parts, n_feat, size, fan), bf),
            pltpu.VMEM((parts, n_feat, size, fan), bf),
            pltpu.VMEM((parts, n_feat, size, fan), bf),
            pltpu.VMEM((parts, n_feat - 1, size, fan), bf),
            dma((2,)), dma((parts,)), dma((parts,)), dma((parts,)), dma((parts,)),
            dma((parts,)), dma((parts,)), dma((parts, n_feat - 1)), dma((parts, n_feat - 1)),
        ],
        compiler_params=pltpu.CompilerParams(collective_id=1, has_side_effects=True, vmem_limit_bytes=40 * MIB),
        name="reduce_dense",
    )(partial_value.reshape(n_col // 2, 2, n_feat, node_dev, fan), weight, bias.reshape(1, hidden))


def solution(mesh):
    placed = (
        P(("row", "col"), "feat"),
        P("row", "col", "feat", None, None),
        P("row", "col", "feat"),
        P("row", "col", "feat"),
        P("row", "col", "feat"),
        P(),
        P(),
    )
    shape = mesh.shape
    return jax.shard_map(
        functools.partial(body, shape["row"], shape["col"], shape["feat"]),
        mesh=mesh, in_specs=placed, out_specs=P(("row", "col", "feat"), None), check_vma=False
    )
```

time: 380 us -> 148 us (0.39)
  waiting for transfers between devices: 279 us -> 0 us
  Pallas kernels: 0 us -> 138 us
  other arithmetic: 31.4 us -> 1.4 us
  blocking collectives: 20.7 us -> 0 us
  local copies, waits for them, and re-layouts: 24.2 us -> 7.42 us
  between operations: 14.1 us -> 0.77 us
  matrix products: 7.64 us -> 0 us
    reduce_scatter x1 -> x0, waiting for transfers between devices: 208 us -> none  [body(): lax.psum_scatter(terms.astype(jnp.bfloat16), ('col', 'feat'), scatter_dim...]
    pallas_call x0 -> x3, Pallas kernels: none -> 138 us  [the longest x1 77.4 us: body(): pl.pallas_call(functools.partial(reduce_kernel, n_feat, parts), out_shape...]
    all_gather x1 -> x0, waiting for transfers between devices: 70.5 us -> none  [body(): sources = lax.all_gather(node_rows, ('row', 'feat'), axis=0, tiled=True)]
    all_to_all x1 -> x0, blocking collectives: 20.7 us -> none  [body(): lax.all_to_all(features, 'feat', split_axis=0, concat_axis=1, tiled=True)]
    scatter-add x3 -> x0, other arithmetic: 18.4 us -> none  [one_turn(): return partial_value.at[rows_here].add(prods)]
    convert_element_type x1 -> x0, other arithmetic: 9.2 us -> none  [body(): partial_value.reshape(block_rows * tile_side, width).astype(jnp.bfloat16)]
    gather x3 -> x0, local copies, waits for them, and re-layouts: 8.81 us -> none  [one_turn(): picked = jnp.take(src_blocks, cols_here, axis=0)]
    broadcast_in_dim x1 -> x0, local copies, waits for them, and re-layouts: 7.85 us -> none  [body(): empty = jnp.zeros((block_rows, tile_side, width), jnp.float32)]
  transfers between devices with their start and end apart: 2 -> 0, of which waited for: 2 -> 0; matrix products, arithmetic and copies ran while one was open for 0% -> 0% of each run, Pallas kernels for 0% -> 0%
where the time goes in v1:
time: 148 us
  Pallas kernels  138 us (93%)
  local copies, waits for them, and re-layouts  7.42 us (5%)
    pallas_call x1, Pallas kernels, body(): pl.pallas_call(functools.partial(reduce_kernel, n_feat, parts), out_shape...  77.4 us
    pallas_call x1, Pallas kernels, body(): pl.pallas_call(functools.partial(gather_kernel, n_row, n_feat, parts), ou...  50.9 us
    pallas_call x1, Pallas kernels, body(): pl.pallas_call(functools.partial(tile_kernel, chunk, unroll, brows), out_...  9.81 us
    unnamed x11, local copies, waits for them, and re-layouts  6.54 us

profile of v1, /device:TPU:0, one launch (start us, length us, event | category | flops | bytes accessed | tf_op | source)
XLA Modules:
  0.0 147.8 jit_solution(15702540521241587260)
XLA Ops:
  0.0 0.0 copy-start
  0.7 0.7 reduce.row_ref
  1.4 0.7 reduce.1.col_ref
  2.1 0.0 copy-done
  2.1 0.9 bitcast_bitcast_fusion.own_ref
  3.0 50.9 %gather_sources.1.src_ref = bf16[128,128,128]{2,1,0:T(8,128)(2,1)} custom-call(bf16[64,32,128]{2,1,0:T(8,128)(2,1)} %bitcast_bitcast_fusion.own_ref), custom_call_target="tpu_custom_call" | custom-call | tf_op jit(solution)/shard_map/gather_sources/pallas_call | solution.py:267
  54.0 0.0 copy-start.2
  54.0 2.2 %copy-done.2 = bf16[128,128,128]{2,1,0:T(8,128)(2,1)S(1)} copy-done((bf16[128,128,128]{2,1,0:T(8,128)(2,1)S(1)}, bf16[128,128,128]{2,1,0:T(8,128)(2,1)}, u32[]{:S(2)}) %copy-start.2) | copy-done | bytes 4194328
  56.1 0.0 copy-start.3
  56.1 0.0 copy-start.4
  56.1 9.8 %tile_products.1 = bf16[256,128,128]{2,1,0:T(8,128)(2,1)} custom-call(s32[1]{0:T(128)} %bitcast.11.count_ref, s32[384]{0:T(512)S(1)} %reduce.row_ref, s32[384]{0:T(512)S(1)} %reduce.1.col_ref, bf16[128,128,128]{2,1,0:T(8,128)(2,1)S(1)} %copy-done.2, bf16[384,128,128]{2,1,0:T(8,128)(2,1)} %bitcast.14), custom_call_target="tpu_custom_call" | custom-call | tf_op jit(solution)/shard_map/tile_products/pallas_call | solution.py:281
  66.0 0.0 copy-done.3
  66.0 0.0 copy-done.4
  66.0 0.0 copy-start.1
  66.0 3.4 %copy-done.1 = bf16[256,128,128]{2,1,0:T(8,128)(2,1)S(1)} copy-done((bf16[256,128,128]{2,1,0:T(8,128)(2,1)S(1)}, bf16[256,128,128]{2,1,0:T(8,128)(2,1)}, u32[]{:S(2)}) %copy-start.1) | copy-done | bytes 8388632
  69.4 77.4 %reduce_dense.1 = bf16[2048,256]{1,0:T(8,128)(2,1)S(1)} custom-call(bf16[2,2,4,2048,128]{4,3,2,1,0:T(8,128)(2,1)S(1)} %bitcast.12, bf16[128,256]{1,0:T(8,128)(2,1)S(1)} %copy-done.3, f32[1,256]{1,0:T(1,128)S(1)} %bitcast.13), custom_call_target="tpu_custom_call" | custom-call | tf_op jit(solution)/shard_map/reduce_dense/pallas_call | solution.py:305
  146.8 1.0 copy.13
Async XLA Ops:
  0.0 2.1 %copy-start = (bf16[8192,32]{0,1:T(8,128)(2,1)S(1)}, bf16[8192,32]{0,1:T(8,128)(2,1)}, u32[]{:S(2)}) copy-start(bf16[8192,32]{0,1:T(8,128)(2,1)} %param.7) | copy-start | bytes 1572868
  54.0 2.2 %copy-start.2 = (bf16[128,128,128]{2,1,0:T(8,128)(2,1)S(1)}, bf16[128,128,128]{2,1,0:T(8,128)(2,1)}, u32[]{:S(2)}) copy-start(bf16[128,128,128]{2,1,0:T(8,128)(2,1)} %gather_sources.1.src_ref) | copy-start | bytes 12582916
  56.1 9.8 %copy-start.3 = (bf16[128,256]{1,0:T(8,128)(2,1)S(1)}, bf16[128,256]{1,0:T(8,128)(2,1)}, u32[]{:S(2)}) copy-start(bf16[128,256]{1,0:T(8,128)(2,1)} %weight_ref.1) | copy-start | bytes 196612
  56.1 9.8 %copy-start.4 = (f32[256]{0:T(256)S(1)}, f32[256]{0:T(256)}, u32[]{:S(2)}) copy-start(f32[256]{0:T(256)} %param.13) | copy-start | bytes 3076
  66.0 3.4 %copy-start.1 = (bf16[256,128,128]{2,1,0:T(8,128)(2,1)S(1)}, bf16[256,128,128]{2,1,0:T(8,128)(2,1)}, u32[]{:S(2)}) copy-start(bf16[256,128,128]{2,1,0:T(8,128)(2,1)} %tile_products.1) | copy-start | bytes 25165828

commit v2 on v1

--- a/solution.py
+++ b/solution.py
@@ -263,7 +263,7 @@
     dma = pltpu.SemaphoreType.DMA
 
     own = features.reshape(blocks, side, width).transpose(0, 2, 1)
-    parts = 4
+    parts = 8
     sources = pl.pallas_call(
         functools.partial(gather_kernel, n_row, n_feat, parts),
         out_shape=jax.ShapeDtypeStruct((n_row * blocks, fan, side), jnp.bfloat16),
@@ -295,7 +295,7 @@
                 dma((2,)),
             ],
         ),
-        compiler_params=pltpu.CompilerParams(vmem_limit_bytes=48 * MIB),
+        compiler_params=pltpu.CompilerParams(vmem_limit_bytes=60 * MIB),
         name="tile_products",
     )(tile_count.reshape(1), tile_row.reshape(slots), tile_col.reshape(slots), sources, tiles.reshape(slots, side, side))
 
@@ -319,7 +319,7 @@
             dma((2,)), dma((parts,)), dma((parts,)), dma((parts,)), dma((parts,)),
             dma((parts,)), dma((parts,)), dma((parts, n_feat - 1)), dma((parts, n_feat - 1)),
         ],
-        compiler_params=pltpu.CompilerParams(collective_id=1, has_side_effects=True, vmem_limit_bytes=40 * MIB),
+        compiler_params=pltpu.CompilerParams(collective_id=1, has_side_effects=True, vmem_limit_bytes=60 * MIB),
         name="reduce_dense",
     )(partial_value.reshape(n_col // 2, 2, n_feat, node_dev, fan), weight, bias.reshape(1, hidden))
 

time: 148 us -> 149 us (level)
  local copies, waits for them, and re-layouts: 7.42 us -> 3.15 us
  Pallas kernels: 138 us -> 141 us
    unnamed x11 -> x3, local copies, waits for them, and re-layouts: 6.54 us -> 2.27 us
where the time goes in v2:
time: 149 us; the launch traced here: 148 us
  Pallas kernels  141 us (95%)
  local copies, waits for them, and re-layouts  3.15 us (2%)
  other arithmetic  2.57 us (2%)
    pallas_call x1, Pallas kernels, body(): pl.pallas_call(functools.partial(reduce_kernel, n_feat, parts), out_shape...  78.3 us
    pallas_call x1, Pallas kernels, body(): pl.pallas_call(functools.partial(gather_kernel, n_row, n_feat, parts), ou...  51.7 us
    pallas_call x1, Pallas kernels, body(): pl.pallas_call(functools.partial(tile_kernel, chunk, unroll, brows), out_...  11.3 us

profile of v2, /device:TPU:0, one launch (start us, length us, event | category | flops | bytes accessed | tf_op | source)
XLA Modules:
  0.0 147.6 jit_solution(9920650385108834883)
XLA Ops:
  0.0 0.0 copy-start
  0.7 1.3 reduce.row_ref
  2.0 1.3 reduce.1.col_ref
  3.3 0.0 copy-done
  3.3 0.9 bitcast_bitcast_fusion.own_ref
  4.2 51.7 %gather_sources.1.src_ref = bf16[128,128,128]{2,1,0:T(8,128)(2,1)} custom-call(bf16[64,32,128]{2,1,0:T(8,128)(2,1)} %bitcast_bitcast_fusion.own_ref), custom_call_target="tpu_custom_call" | custom-call | tf_op jit(solution)/shard_map/gather_sources/pallas_call | solution.py:267
  55.8 11.3 %tile_products.1 = bf16[256,128,128]{2,1,0:T(8,128)(2,1)} custom-call(s32[1]{0:T(128)} %bitcast.11.count_ref, s32[384]{0:T(512)} %reduce.row_ref, s32[384]{0:T(512)} %reduce.1.col_ref, bf16[128,128,128]{2,1,0:T(8,128)(2,1)} %gather_sources.1.src_ref, bf16[384,128,128]{2,1,0:T(8,128)(2,1)} %bitcast.13), custom_call_target="tpu_custom_call" | custom-call | tf_op jit(solution)/shard_map/tile_products/pallas_call | solution.py:281
  67.1 78.3 %reduce_dense.1 = bf16[2048,256]{1,0:T(8,128)(2,1)} custom-call(bf16[2,2,4,2048,128]{4,3,2,1,0:T(8,128)(2,1)} %bitcast.12, bf16[128,256]{1,0:T(8,128)(2,1)} %weight_ref.1, f32[1,256]{1,0:T(1,128)} %bitcast.14), custom_call_target="tpu_custom_call" | custom-call | tf_op jit(solution)/shard_map/reduce_dense/pallas_call | solution.py:305
  145.4 2.3 %copy.13 = bf16[2048,256]{1,0:T(8,128)(2,1)} copy(bf16[2048,256]{1,0:T(8,128)(2,1)} %reduce_dense.1) | data formatting | bytes 2097152
Async XLA Ops:
  0.0 3.3 %copy-start = (bf16[8192,32]{0,1:T(8,128)(2,1)S(1)}, bf16[8192,32]{0,1:T(8,128)(2,1)}, u32[]{:S(2)}) copy-start(bf16[8192,32]{0,1:T(8,128)(2,1)} %param.7) | copy-start | bytes 1572868

commit v3 on v1

--- a/solution.py
+++ b/solution.py
@@ -295,7 +295,7 @@
                 dma((2,)),
             ],
         ),
-        compiler_params=pltpu.CompilerParams(vmem_limit_bytes=48 * MIB),
+        compiler_params=pltpu.CompilerParams(vmem_limit_bytes=60 * MIB),
         name="tile_products",
     )(tile_count.reshape(1), tile_row.reshape(slots), tile_col.reshape(slots), sources, tiles.reshape(slots, side, side))
 

time: 148 us -> 149 us (level)
  local copies, waits for them, and re-layouts: 7.42 us -> 5.25 us
  Pallas kernels: 138 us -> 140 us
    pallas_call x1, Pallas kernels: 9.81 us -> 18.8 us  [body(): pl.pallas_call(functools.partial(tile_kernel, chunk, unroll, brows), out_...]
    pallas_call x1, Pallas kernels: 77.4 us -> 70.5 us  [body(): pl.pallas_call(functools.partial(reduce_kernel, n_feat, parts), out_shape...]
    unnamed x11 -> x9, local copies, waits for them, and re-layouts: 6.54 us -> 4.36 us
where the time goes in v3:
time: 149 us
  Pallas kernels  140 us (94%)
  local copies, waits for them, and re-layouts  5.25 us (4%)
  other arithmetic  2.57 us (2%)
    pallas_call x1, Pallas kernels, body(): pl.pallas_call(functools.partial(reduce_kernel, n_feat, parts), out_shape...  70.5 us
    pallas_call x1, Pallas kernels, body(): pl.pallas_call(functools.partial(gather_kernel, n_row, n_feat, parts), ou...  50.9 us
    pallas_call x1, Pallas kernels, body(): pl.pallas_call(functools.partial(tile_kernel, chunk, unroll, brows), out_...  18.8 us
    unnamed x9, local copies, waits for them, and re-layouts  4.36 us

profile of v3, /device:TPU:0, one launch (start us, length us, event | category | flops | bytes accessed | tf_op | source)
XLA Modules:
  0.0 148.9 jit_solution(15328044058670728693)
XLA Ops:
  0.0 0.0 copy-start
  0.7 1.3 reduce.row_ref
  2.0 1.3 reduce.1.col_ref
  3.3 0.0 copy-done
  3.3 0.9 bitcast_bitcast_fusion.own_ref
  4.2 50.9 %gather_sources.1.src_ref = bf16[128,128,128]{2,1,0:T(8,128)(2,1)} custom-call(bf16[64,32,128]{2,1,0:T(8,128)(2,1)} %bitcast_bitcast_fusion.own_ref), custom_call_target="tpu_custom_call" | custom-call | tf_op jit(solution)/shard_map/gather_sources/pallas_call | solution.py:267
  55.1 0.0 copy-start.2
  55.1 0.0 copy-start.3
  55.1 18.8 %tile_products.1 = bf16[256,128,128]{2,1,0:T(8,128)(2,1)} custom-call(s32[1]{0:T(128)} %bitcast.11.count_ref, s32[384]{0:T(512)} %reduce.row_ref, s32[384]{0:T(512)} %reduce.1.col_ref, bf16[128,128,128]{2,1,0:T(8,128)(2,1)} %gather_sources.1.src_ref, bf16[384,128,128]{2,1,0:T(8,128)(2,1)} %bitcast.14), custom_call_target="tpu_custom_call" | custom-call | tf_op jit(solution)/shard_map/tile_products/pallas_call | solution.py:281
  74.0 0.0 copy-done.2
  74.0 0.0 copy-done.3
  74.0 0.0 copy-start.1
  74.0 3.4 %copy-done.1 = bf16[256,128,128]{2,1,0:T(8,128)(2,1)S(1)} copy-done((bf16[256,128,128]{2,1,0:T(8,128)(2,1)S(1)}, bf16[256,128,128]{2,1,0:T(8,128)(2,1)}, u32[]{:S(2)}) %copy-start.1) | copy-done | bytes 8388632
  77.4 70.5 %reduce_dense.1 = bf16[2048,256]{1,0:T(8,128)(2,1)S(1)} custom-call(bf16[2,2,4,2048,128]{4,3,2,1,0:T(8,128)(2,1)S(1)} %bitcast.12, bf16[128,256]{1,0:T(8,128)(2,1)S(1)} %copy-done.2, f32[1,256]{1,0:T(1,128)S(1)} %bitcast.13), custom_call_target="tpu_custom_call" | custom-call | tf_op jit(solution)/shard_map/reduce_dense/pallas_call | solution.py:305
  147.9 1.0 copy.13
Async XLA Ops:
  0.0 3.3 %copy-start = (bf16[8192,32]{0,1:T(8,128)(2,1)S(1)}, bf16[8192,32]{0,1:T(8,128)(2,1)}, u32[]{:S(2)}) copy-start(bf16[8192,32]{0,1:T(8,128)(2,1)} %param.7) | copy-start | bytes 1572868
  55.1 18.8 %copy-start.2 = (bf16[128,256]{1,0:T(8,128)(2,1)S(1)}, bf16[128,256]{1,0:T(8,128)(2,1)}, u32[]{:S(2)}) copy-start(bf16[128,256]{1,0:T(8,128)(2,1)} %weight_ref.1) | copy-start | bytes 196612
  55.1 18.8 %copy-start.3 = (f32[256]{0:T(256)S(1)}, f32[256]{0:T(256)}, u32[]{:S(2)}) copy-start(f32[256]{0:T(256)} %param.13) | copy-start | bytes 3076
  74.0 3.4 %copy-start.1 = (bf16[256,128,128]{2,1,0:T(8,128)(2,1)S(1)}, bf16[256,128,128]{2,1,0:T(8,128)(2,1)}, u32[]{:S(2)}) copy-start(bf16[256,128,128]{2,1,0:T(8,128)(2,1)} %tile_products.1) | copy-start | bytes 25165828

commit v4 on v3

--- a/solution.py
+++ b/solution.py
@@ -116,7 +116,7 @@
         def clear(b, carry):
             acc[b] = jnp.zeros(acc.shape[1:], jnp.float32)
             return carry
-        lax.fori_loop(0, brows, clear, 0)
+        lax.fori_loop(0, brows, clear, 0, unroll=4)
 
     left = count - i * chunk
     turns = jnp.clip((left + unroll - 1) // unroll, 0, chunk // unroll)
@@ -144,7 +144,7 @@
             def cast(b, carry):
                 stage[n % 2, b] = acc[n * size + b].astype(jnp.bfloat16)
                 return carry
-            lax.fori_loop(0, size, cast, 0)
+            lax.fori_loop(0, size, cast, 0, unroll=4)
             put(n).start()
         for n in range(max(0, total - 2), total):
             put(n).wait()
@@ -277,7 +277,7 @@
         name="gather_sources",
     )(own)
 
-    chunk, unroll = 32, 8
+    chunk, unroll = 32, 16
     partial_value = pl.pallas_call(
         functools.partial(tile_kernel, chunk, unroll, brows),
         out_shape=jax.ShapeDtypeStruct((brows, side, fan), jnp.bfloat16),

time: 149 us -> 146 us (0.980)
  Pallas kernels: 140 us -> 137 us
    pallas_call x1, Pallas kernels: 70.5 us -> 63.5 us  [body(): pl.pallas_call(functools.partial(reduce_kernel, n_feat, parts), out_shape...]
    pallas_call x1, Pallas kernels: 18.8 us -> 22.7 us  [body(): pl.pallas_call(functools.partial(tile_kernel, chunk, unroll, brows), out_...]
where the time goes in v4:
time: 146 us
  Pallas kernels  137 us (94%)
  local copies, waits for them, and re-layouts  5.25 us (4%)
  other arithmetic  2.57 us (2%)
    pallas_call x1, Pallas kernels, body(): pl.pallas_call(functools.partial(reduce_kernel, n_feat, parts), out_shape...  63.5 us
    pallas_call x1, Pallas kernels, body(): pl.pallas_call(functools.partial(gather_kernel, n_row, n_feat, parts), ou...  50.9 us
    pallas_call x1, Pallas kernels, body(): pl.pallas_call(functools.partial(tile_kernel, chunk, unroll, brows), out_...  22.7 us
    unnamed x9, local copies, waits for them, and re-layouts  4.36 us

profile of v4, /device:TPU:0, one launch (start us, length us, event | category | flops | bytes accessed | tf_op | source)
XLA Modules:
  0.0 145.8 jit_solution(9768697799870285825)
XLA Ops:
  0.0 0.0 copy-start
  0.7 1.3 reduce.row_ref
  2.0 1.3 reduce.1.col_ref
  3.3 0.0 copy-done
  3.3 0.9 bitcast_bitcast_fusion.own_ref
  4.2 50.9 %gather_sources.1.src_ref = bf16[128,128,128]{2,1,0:T(8,128)(2,1)} custom-call(bf16[64,32,128]{2,1,0:T(8,128)(2,1)} %bitcast_bitcast_fusion.own_ref), custom_call_target="tpu_custom_call" | custom-call | tf_op jit(solution)/shard_map/gather_sources/pallas_call | solution.py:267
  55.1 0.0 copy-start.2
  55.1 0.0 copy-start.3
  55.1 22.7 %tile_products.1 = bf16[256,128,128]{2,1,0:T(8,128)(2,1)} custom-call(s32[1]{0:T(128)} %bitcast.11.count_ref, s32[384]{0:T(512)} %reduce.row_ref, s32[384]{0:T(512)} %reduce.1.col_ref, bf16[128,128,128]{2,1,0:T(8,128)(2,1)} %gather_sources.1.src_ref, bf16[384,128,128]{2,1,0:T(8,128)(2,1)} %bitcast.14), custom_call_target="tpu_custom_call" | custom-call | tf_op jit(solution)/shard_map/tile_products/pallas_call | solution.py:281
  77.9 0.0 copy-done.2
  77.9 0.0 copy-done.3
  77.9 0.0 copy-start.1
  77.9 3.4 %copy-done.1 = bf16[256,128,128]{2,1,0:T(8,128)(2,1)S(1)} copy-done((bf16[256,128,128]{2,1,0:T(8,128)(2,1)S(1)}, bf16[256,128,128]{2,1,0:T(8,128)(2,1)}, u32[]{:S(2)}) %copy-start.1) | copy-done | bytes 8388632
  81.3 63.5 %reduce_dense.1 = bf16[2048,256]{1,0:T(8,128)(2,1)S(1)} custom-call(bf16[2,2,4,2048,128]{4,3,2,1,0:T(8,128)(2,1)S(1)} %bitcast.12, bf16[128,256]{1,0:T(8,128)(2,1)S(1)} %copy-done.2, f32[1,256]{1,0:T(1,128)S(1)} %bitcast.13), custom_call_target="tpu_custom_call" | custom-call | tf_op jit(solution)/shard_map/reduce_dense/pallas_call | solution.py:305
  144.8 1.0 copy.13
Async XLA Ops:
  0.0 3.3 %copy-start = (bf16[8192,32]{0,1:T(8,128)(2,1)S(1)}, bf16[8192,32]{0,1:T(8,128)(2,1)}, u32[]{:S(2)}) copy-start(bf16[8192,32]{0,1:T(8,128)(2,1)} %param.7) | copy-start | bytes 1572868
  55.1 22.8 %copy-start.2 = (bf16[128,256]{1,0:T(8,128)(2,1)S(1)}, bf16[128,256]{1,0:T(8,128)(2,1)}, u32[]{:S(2)}) copy-start(bf16[128,256]{1,0:T(8,128)(2,1)} %weight_ref.1) | copy-start | bytes 196612
  55.1 22.8 %copy-start.3 = (f32[256]{0:T(256)S(1)}, f32[256]{0:T(256)}, u32[]{:S(2)}) copy-start(f32[256]{0:T(256)} %param.13) | copy-start | bytes 3076
  77.9 3.4 %copy-start.1 = (bf16[256,128,128]{2,1,0:T(8,128)(2,1)S(1)}, bf16[256,128,128]{2,1,0:T(8,128)(2,1)}, u32[]{:S(2)}) copy-start(bf16[256,128,128]{2,1,0:T(8,128)(2,1)} %tile_products.1) | copy-start | bytes 25165828
